TPU v7x, 128 devices: a whole 4x4x4 slice. The times are simulated.
128 devices in a mesh: prompt: 4 (over y), resp: 32 (over x, z, core).
Axes of the slice: x: 4, y: 4, z: 4, core: 2. Of those that a mesh axis runs over, the one named last changes fastest.
Arguments:
- queries: bfloat16 [16384, 64, 576], P(('prompt', 'resp')), may hold values from -340 to 340
- d_output: bfloat16 [16384, 64, 512], P(('prompt', 'resp')), may hold values from -6 to 6
- resp_latent: bfloat16 [16384, 576], P(('prompt', 'resp')), may hold values from -7 to 7
- prompt_latent: bfloat16 [8, 384, 576], P(None, 'prompt'), may hold values from -6 to 6
- assignment: int32 [128], replicated, may hold values from 0 to 127, each once
- lengths: int32 [128], P(('prompt', 'resp')), may hold values from 32 to 128
Outputs:
- d_prompt_latent: float32 [8, 384, 576], P(None, ('prompt', 'resp'))
- d_resp_latent: float32 [16384, 576], P(('prompt', 'resp'))
All inputs are finite; a program needn't handle non-finite values.
Results may differ from a plain program's by a relative error of at most 0.014.
Values may be sent and summed in bfloat16 or wider, within the bound.
A program may use at most 192 MiB of HBM per device.

v0:
```python
import jax
import jax.numpy as jnp
from jax import lax
from jax.sharding import PartitionSpec as P

DC = 512
QK_DIM = 192
GROUP = 16


def attend_grads(queries, d_output, keys, length):
    rows = queries.shape[0]
    total = keys.shape[0]
    scale = QK_DIM ** (-0.5)
    scores = jnp.einsum("thk,sk->ths", queries, keys, preferred_element_type=jnp.float32) * scale
    position = jnp.arange(rows)[:, None]
    key_pos = jnp.arange(total)[None, :] - (total - rows)
    allowed = key_pos <= position
    scores = jnp.where(allowed[:, None, :], scores, -jnp.inf)
    top = jnp.max(scores, axis=-1, keepdims=True)
    expo = jnp.exp(scores - top)
    probs = expo / jnp.sum(expo, axis=-1, keepdims=True)
    probs_b = probs.astype(jnp.bfloat16)
    values = keys[:, :DC]
    output = jnp.einsum("ths,sc->thc", probs_b, values, preferred_element_type=jnp.float32)
    live = jnp.arange(rows) < length
    grads = jnp.where(live[:, None, None], d_output, jnp.zeros_like(d_output))
    dprobs = jnp.einsum("thc,sc->ths", grads, values, preferred_element_type=jnp.float32)
    delta = jnp.sum(grads.astype(jnp.float32) * output, axis=-1)
    dscores = (probs * (dprobs - delta[..., None])).astype(jnp.bfloat16)
    dkeys = scale * jnp.einsum("ths,thk->sk", dscores, queries, preferred_element_type=jnp.float32)
    dvalues = jnp.einsum("ths,thc->sc", probs_b, grads, preferred_element_type=jnp.float32)
    return dkeys + jnp.pad(dvalues, ((0, 0), (0, keys.shape[1] - DC)))


def body(queries, d_output, resp_latent, prompt_latent, assignment, lengths):
    resp_count = lax.axis_size("resp")
    prompt_place = lax.axis_index("prompt")
    resp_place = lax.axis_index("resp")
    device = prompt_place * resp_count + resp_place
    nprompt = prompt_latent.shape[0]
    prompt_ids = assignment // GROUP
    my_prompt = lax.dynamic_index_in_dim(prompt_ids, device, 0, keepdims=False)
    everything = lax.all_gather(prompt_latent, "prompt", axis=1, tiled=True)
    context = lax.dynamic_index_in_dim(everything, my_prompt, 0, keepdims=False)
    prompt_len = context.shape[0]
    keys = jnp.concatenate([context, resp_latent], axis=0)
    dkeys = attend_grads(queries, d_output, keys, lengths[0])
    d_resp = dkeys[prompt_len:]
    d_context = dkeys[:prompt_len]
    onehot = (jnp.arange(nprompt) == my_prompt).astype(jnp.float32)
    spread = onehot[:, None, None] * d_context[None]
    d_prompt = lax.psum_scatter(spread, ("prompt", "resp"), scatter_dimension=1, tiled=True)
    return (d_prompt, d_resp)


def solution(mesh):
    in_specs = (
        P(("prompt", "resp"), None, None),
        P(("prompt", "resp"), None, None),
        P(("prompt", "resp"), None),
        P(None, "prompt", None),
        P(),
        P(("prompt", "resp")),
    )
    out_specs = (P(None, ("prompt", "resp"), None), P(("prompt", "resp"), None))
    return jax.shard_map(body, mesh=mesh, in_specs=in_specs, out_specs=out_specs, check_vma=False)
```

profile of v0, /device:TPU:1, one launch (start us, length us, event | category | flops | bytes accessed | tf_op | source)
XLA Modules:
  0.0 381.5 jit_solution(768730704146210927)
XLA Ops:
  7.2 0.0 all-gather.2.cloned.1.call-start
  7.2 0.7 all-gather.2.cloned.1.call-update
  7.9 0.0 reduce-scatter.4.cloned.1.call-start
  8.6 7.2 %broadcast_select_fusion = bf16[128,64,512]{2,1,0:T(8,128)(2,1)} fusion(bf16[128,64,512]{2,1,0:T(8,128)(2,1)} %param.7, pred[128]{0:T(512)(128)(4,1)S(1)} %iota_compare_fusion.1), kind=kLoop, calls=%fused_computation.9 | loop fusion | flops 4194304 | bytes 16777344 | tf_op jit(solution)/shard_map/jit(_where)/select_n | solution.py:27
  15.8 13.2 %copy.17 = bf16[128,64,512]{0,2,1:T(8,128)(2,1)} copy(bf16[128,64,512]{2,1,0:T(8,128)(2,1)} %broadcast_select_fusion) | data formatting | bytes 16777216 | tf_op jit(solution)/shard_map/jit(_where)/select_n | solution.py:27
  29.1 0.6 dynamic_slice.8
  31.6 0.6 compare_convert_fusion
  32.3 0.1 iota_compare_fusion
  32.4 26.6 %all-gather.2.cloned.1.call-done = bf16[8,384,576]{2,1,0:T(8,128)(2,1)} async-done(((bf16[8,96,576]{2,1,0:T(8,128)(2,1)}), bf16[8,384,576]{2,1,0:T(8,128)(2,1)}) %all-gather.2.cloned.1.call-update) | async-done | bytes 3538960 | tf_op jit(solution)/shard_map/all_gather | solution.py:44
  59.0 1.1 constant_dynamic-slice_fusion
  60.0 0.2 copy.13
  60.3 13.9 %fusion.11 = f32[512,128,64]{1,0,2:T(8,128)} fusion(bf16[128,64,576]{0,2,1:T(8,128)(2,1)} %param.6, bf16[128,576]{0,1:T(8,128)(2,1)S(1)} %copy-done, bf16[384,576]{0,1:T(8,128)(2,1)S(1)} %bitcast.37), kind=kOutput, calls=%fused_computation.22 | convolution fusion | flops 4833017856 | bytes 26804224 | tf_op jit(solution)/shard_map/thk,sk->ths/dot_general | solution.py:15
  74.2 19.7 %fusion.24 = (f32[128,64]{0,1:T(8,128)S(1)}, f32[128,64,512]{0,2,1:T(8,128)}) fusion(f32[512,128,64]{1,0,2:T(8,128)} %fusion.11, pred[128,512]{0,1:T(8,128)(4,1)S(1)} %iota_compare_fusion), kind=kOutput, calls=%fused_computation.39 | output fusion | flops 25166336 | bytes 33652736 | tf_op jit(solution)/shard_map/sub | solution.py:21
  93.8 9.5 %fusion.5 = bf16[128,64,512]{0,2,1:T(8,128)(2,1)} fusion(f32[128,64,512]{0,2,1:T(8,128)} %get-tuple-element.3, f32[128,64]{0,1:T(8,128)S(1)} %get-tuple-element.2), kind=kLoop, calls=%fused_computation.11 | loop fusion | flops 8388608 | bytes 25198592 | tf_op jit(solution)/shard_map/convert_element_type | solution.py:23
  103.3 12.6 %copy.20 = bf16[128,64,512]{2,1,0:T(8,128)(2,1)} copy(bf16[128,64,512]{0,2,1:T(8,128)(2,1)} %fusion.5) | data formatting | bytes 16777216 | tf_op jit(solution)/shard_map/convert_element_type | solution.py:23
  115.9 9.8 %multiply_reduce_fusion = f32[128,64]{1,0:T(8,128)S(1)} fusion(bf16[128,64,512]{2,1,0:T(8,128)(2,1)} %broadcast_select_fusion, bf16[128,64,512]{2,1,0:T(8,128)(2,1)} %copy.20, bf16[384,576]{0,1:T(8,128)(2,1)S(1)} %bitcast.38, bf16[128,576]{0,1:T(8,128)(2,1)S(1)} %copy-done), kind=kOutput, calls=%fused_computation.3 | convolution fusion | flops 4308590592 | bytes 17399808 | tf_op jit(solution)/shard_map/ths,sc->thc/dot_general | solution.py:25
  125.7 0.1 copy.14
  125.7 11.4 %convolution_bitcast_fusion = f32[512,512]{0,1:T(8,128)} fusion(bf16[128,64,512]{0,2,1:T(8,128)(2,1)} %fusion.5, bf16[128,64,512]{0,2,1:T(8,128)(2,1)} %copy.17), kind=kOutput, calls=%fused_computation.17 | convolution fusion | flops 4294967296 | bytes 17825792 | tf_op jit(solution)/shard_map/ths,thc->sc/dot_general | solution.py:32
  137.1 19.2 %fusion.9 = f32[512,576]{0,1:T(8,128)S(1)} fusion(bf16[128,64,576]{0,2,1:T(8,128)(2,1)} %param.6, bf16[128,64,512]{0,2,1:T(8,128)(2,1)} %copy.17, f32[128,64]{0,1:T(8,128)S(1)} %copy.14, f32[128,64,512]{0,2,1:T(8,128)} %get-tuple-element.3, f32[128,64]{0,1:T(8,128)S(1)} %get-tuple-element.2, f32[512,512]{0,1:T(8,128)} %convolution_bitcast_fusion, ...), kind=kOutput, calls=%fused_computation.16 | convolution fusion | flops 9145221120 | bytes 37486592 | tf_op jit(solution)/shard_map/ths,thk->sk/dot_general | solution.py:31
  156.3 0.1 slice.14
  156.4 0.3 copy.18
  156.7 3.7 broadcast_multiply_fusion
  160.4 0.8 slice.15
  161.2 213.5 %reduce-scatter.4.cloned.1.call-done = f32[8,3,576]{2,0,1:T(8,128)} async-done(((f32[8,384,576]{2,0,1:T(8,128)}), f32[8,3,576]{2,0,1:T(8,128)}) %reduce-scatter.4.cloned.1.call-update) | async-done | bytes 55312
  (8 shorter events, 0.0 us)
Async XLA Ops:
  7.2 51.8 %all-gather.2.cloned.1.call-start = ((), (), s32[]{:S(2)}) async-start(), calls=%async_computation.1 | async-start | bytes 4915200 | tf_op jit(solution)/shard_map/all_gather | solution.py:44
  7.9 366.7 %reduce-scatter.4.cloned.1.call-start = ((), (), s32[]{:S(2)}) async-start(), calls=%async_computation.2 | async-start | bytes 7925760
  15.8 13.2 %copy-start.1 = (s32[128]{0:T(128)S(1)}, s32[128]{0:T(128)}, u32[]{:S(2)}) copy-start(s32[128]{0:T(128)} %param.10) | copy-start | bytes 1540
  15.8 44.5 %copy-start = (bf16[128,576]{0,1:T(8,128)(2,1)S(1)}, bf16[128,576]{0,1:T(8,128)(2,1)}, u32[]{:S(2)}) copy-start(bf16[128,576]{0,1:T(8,128)(2,1)} %param.8) | copy-start | bytes 442372
Sparse Core Ops, SparseCore 0:
  9.7 49.2 all-gather.1
  160.5 214.0 reduce-scatter.3
where the time goes:
time: 383 us; the launch traced here: 381 us
  waiting for transfers between devices  241 us (63%)
  matrix products  54.2 us (14%)
  other arithmetic  40.8 us (11%)
  local copies, waits for them, and re-layouts  29 us (8%)
  between operations  16.7 us (4%)
    unnamed x3, waiting for transfers between devices  214 us
    all_gather x1, waiting for transfers between devices, body(): everything = lax.all_gather(prompt_latent, 'prompt', axis=1, tiled=True)  26.6 us
    sub x1, other arithmetic, attend_grads(): expo = jnp.exp(scores - top)  19.7 us
    dot_general x1, matrix products, attend_grads(): jnp.einsum('ths,thk->sk', dscores, queries, preferred_element_type=jnp.fl...  19.2 us
    dot_general x1, matrix products, attend_grads(): jnp.einsum('thk,sk->ths', queries, keys, preferred_element_type=jnp.float32)  13.9 us
    select_n x1, local copies, waits for them, and re-layouts, attend_grads(): grads = jnp.where(live[:, None, None], d_output, jnp.zeros_like(d_output))  13.2 us
    convert_element_type x1, local copies, waits for them, and re-layouts, attend_grads(): probs_b = probs.astype(jnp.bfloat16)  12.6 us
    dot_general x1, matrix products, attend_grads(): jnp.einsum('ths,thc->sc', probs_b, grads, preferred_element_type=jnp.floa...  11.4 us
  transfers between devices with their start and end apart: 2, of which 2 were waited for; matrix products, arithmetic and copies ran while one was open for 6% of the time, Pallas kernels for 0%

commit v1 on v0

v1 whole, which is shorter than its diff:
```python
import functools
import math

import jax
import jax.numpy as jnp
from jax import lax
from jax.experimental import pallas as pl
from jax.experimental.pallas import tpu as pltpu
from jax.sharding import PartitionSpec as P

BF = jnp.bfloat16
F32 = jnp.float32
DC = 512
KD = 576
HEADS = 64
GROUP = 16
RLEN = 128
PLEN = 384
NPROMPT = 8
SCALE = 192 ** -0.5
EXP2_SCALE = SCALE * math.log2(math.e)
MASKED = -1e38
NY, NR = 4, 32
NDEV = NY * NR
SHARD = PLEN // NY
OWN = PLEN // NDEV
KEYS = PLEN + RLEN
G = 4
COLS = G * RLEN
STEPS = HEADS // G
W = 4
MESH = pl.DeviceIdType.MESH


def dot(a, b, on):
    return lax.dot_general(a, b, (on, ((), ())), preferred_element_type=F32)


NN = ((1,), (0,))
NT = ((1,), (1,))


def coords(device):
    return (device // NR, lax.rem(device, NR))


def kernel(
    q_hbm, do_hbm, prompt_hbm, resp_ref, assign_ref, assign_row, len_ref,
    dprompt_ref, dresp_ref,
    q, do_v, do_t, prompt, keys, sendk, s0, s1, d0, d1, p_ref, ds_ref, acc,
    rows, msg32, msg, recv, pick, summed,
    load_sem, do_sem, prompt_sem, ksend_sem, krecv_sem, msend_sem, mrecv_sem,
):
    y = lax.axis_index("prompt")
    r = lax.axis_index("resp")
    me = y * NR + r

    q_load = pltpu.make_async_copy(q_hbm, q, load_sem)
    prompt_load = pltpu.make_async_copy(prompt_hbm, prompt, prompt_sem)
    prompt_load.start()

    def do_load(g):
        heads = pl.ds(pl.multiple_of(g * 16, 16), 16)
        return pltpu.make_async_copy(do_hbm.at[:, heads], do_v.at[:, heads], do_sem.at[g])

    for g in range(4):
        do_load(g).start()
    q_load.start()

    barrier = pltpu.get_barrier_semaphore()

    def greet(step, carry):
        other = lax.rem(me + step, NDEV)
        pl.semaphore_signal(barrier, inc=1, device_id=coords(other), device_id_type=MESH)
        return carry

    lax.fori_loop(1, NDEV, greet, 0)

    prompt_load.wait()
    keys[pl.ds(pl.multiple_of(y * SHARD, 16), SHARD), :] = prompt[assign_ref[me] // GROUP]
    keys[PLEN:KEYS, :] = resp_ref[...].T
    for k in range(1, NY):
        peer = lax.rem(y + k, NY) * NR + r
        sendk[k - 1] = prompt[assign_ref[peer] // GROUP]

    pl.semaphore_wait(barrier, NDEV - 1)

    def key_copy(k):
        return pltpu.make_async_remote_copy(
            src_ref=sendk.at[k - 1],
            dst_ref=keys.at[pl.ds(pl.multiple_of(y * SHARD, 16), SHARD), :],
            send_sem=ksend_sem.at[k - 1],
            recv_sem=krecv_sem.at[k - 1],
            device_id=(lax.rem(y + k, NY), r),
            device_id_type=MESH,
        )

    def key_arrival(k):
        source = lax.rem(y + NY - k, NY)
        return pltpu.make_async_remote_copy(
            src_ref=sendk.at[k - 1],
            dst_ref=keys.at[pl.ds(pl.multiple_of(source * SHARD, 16), SHARD), :],
            send_sem=ksend_sem.at[k - 1],
            recv_sem=krecv_sem.at[k - 1],
            device_id=(lax.rem(y + k, NY), r),
            device_id_type=MESH,
        )

    for k in (2, 1, 3):
        key_copy(k).start()

    def turn(g, carry):
        do_load(g).wait()
        h0 = pl.multiple_of(g * 16, 16)
        x = jnp.concatenate(
            [jnp.swapaxes(do_v[pl.ds(t * 16, 16), pl.ds(h0, 16), :], 0, 1) for t in range(8)], axis=1
        )
        for h in range(16):
            do_t[h0 + h] = x[h].T
        return carry

    lax.fori_loop(0, 4, turn, 0)

    src = lax.broadcasted_iota(jnp.int32, (NDEV, NDEV * 16), 0)
    lane = lax.broadcasted_iota(jnp.int32, (NDEV, NDEV * 16), 1)
    spread = (src == lane // 16).astype(BF)
    pids = jnp.broadcast_to(assign_row[...] // GROUP, (8, NDEV)).astype(BF)
    pid_lane = dot(pids, spread, NN)[0:1]
    row = lax.broadcasted_iota(jnp.int32, (NDEV, NDEV * 16), 0)
    hit = (pid_lane == (row & 7).astype(F32)) & ((row // 8) == (lane & 15))
    pick[...] = hit.astype(BF)

    q_load.wait()
    for k in (1, 2, 3):
        key_arrival(k).wait_recv()

    def qcat(i):
        return jnp.concatenate([q[i * G + h] for h in range(G)], axis=1)

    def dcat(i):
        return jnp.concatenate([do_t[i * G + h] for h in range(G)], axis=1)

    def products(i, s, d):
        s[...] = dot(keys[...], qcat(i), NN)
        d[...] = dot(keys[:, :DC], dcat(i), NN)

    def soft(i, s_ref, d_ref):
        key_pos = lax.broadcasted_iota(jnp.int32, (RLEN, RLEN), 0)
        token = lax.broadcasted_iota(jnp.int32, (RLEN, RLEN), 1)
        allowed = key_pos <= token
        live = lax.broadcasted_iota(jnp.int32, (1, RLEN), 1) < len_ref[0]
        for h in range(G):
            cs = slice(h * RLEN, (h + 1) * RLEN)
            s = s_ref[:, cs]
            s = jnp.concatenate([s[:PLEN], jnp.where(allowed, s[PLEN:], MASKED)], axis=0)
            top = jnp.max(s, axis=0, keepdims=True)
            e = jnp.exp2((s - top) * EXP2_SCALE)
            dp = d_ref[:, cs]
            inv = 1.0 / jnp.sum(e, axis=0, keepdims=True)
            delta = jnp.sum(e * dp, axis=0, keepdims=True) * inv
            inv = jnp.where(live, inv, 0.0)
            p_ref[i, :, cs] = (e * inv).astype(BF)
            ds_ref[i, :, cs] = (e * (inv * SCALE) * (dp - delta)).astype(BF)

    last = STEPS - 1
    products(0, s0, d0)

    def attend(j, carry):
        i = 2 * j
        products(i + 1, s1, d1)
        soft(i, s0, d0)
        products(jnp.minimum(i + 2, last), s0, d0)
        soft(i + 1, s1, d1)
        return carry

    lax.fori_loop(0, STEPS // 2, attend, 0)

    acc[...] = jnp.zeros_like(acc)

    def gradients(j, carry):
        qc = jnp.concatenate([qcat(W * j + w) for w in range(W)], axis=1)
        dc = jnp.concatenate([dcat(W * j + w) for w in range(W)], axis=1)
        ds = jnp.concatenate([ds_ref[W * j + w] for w in range(W)], axis=1)
        p = jnp.concatenate([p_ref[W * j + w] for w in range(W)], axis=1)
        a = dot(qc, ds, NT)
        b = dot(dc, p, NT)
        acc[0:DC, :] += a[:DC] + b
        acc[DC:KD, :] += a[DC:]
        return carry

    lax.fori_loop(0, STEPS // W, gradients, 0)

    for c in range(5):
        rows[c] = acc[c * 128:(c + 1) * 128, 0:PLEN].T
    msg32[pl.ds(15, NDEV, stride=16), :] = jnp.zeros((NDEV, 128), F32)
    for i in range(OWN):
        for c in range(5):
            msg32[pl.ds(i * 5 + c, NDEV, stride=16), :] = rows[c, pl.ds(i, NDEV, stride=OWN), :]
    msg[...] = msg32[...].reshape(NDEV, 16, 128).astype(BF)

    def send(step, carry):
        other = lax.rem(me + step, NDEV)
        pltpu.make_async_remote_copy(
            src_ref=msg.at[other], dst_ref=recv.at[me],
            send_sem=msend_sem, recv_sem=mrecv_sem,
            device_id=coords(other), device_id_type=MESH,
        ).start()
        return carry

    lax.fori_loop(1, NDEV, send, 0)
    recv[me] = msg[me]
    dresp_ref[...] = acc[0:KD, PLEN:KEYS]

    whole = pltpu.make_async_remote_copy(
        src_ref=msg.at[pl.ds(0, NDEV - 1)], dst_ref=recv.at[pl.ds(0, NDEV - 1)],
        send_sem=msend_sem, recv_sem=mrecv_sem,
        device_id=coords(lax.rem(me + 1, NDEV)), device_id_type=MESH,
    )
    whole.wait_recv()
    summed[...] = dot(pick[...], recv[...].reshape(NDEV * 16, 128), NN)
    for i in range(OWN):
        for c in range(5):
            k = i * 5 + c
            width = min(128, KD - c * 128)
            dprompt_ref[i, :, c * 128:c * 128 + width] = summed[k * 8:(k + 1) * 8, 0:width]
    whole.wait_send()
    for k in (1, 2, 3):
        key_copy(k).wait_send()


def body(queries, d_output, resp_latent, prompt_latent, assignment, lengths):
    smem = pl.BlockSpec(memory_space=pltpu.SMEM)
    vmem = pl.BlockSpec(memory_space=pltpu.VMEM)
    hbm = pl.BlockSpec(memory_space=pl.ANY)
    dprompt, dresp = pl.pallas_call(
        kernel,
        out_shape=(
            jax.ShapeDtypeStruct((OWN, NPROMPT, KD), F32),
            jax.ShapeDtypeStruct((KD, RLEN), F32),
        ),
        in_specs=[hbm, hbm, hbm, vmem, smem, vmem, smem],
        out_specs=(vmem, vmem),
        scratch_shapes=[
            pltpu.VMEM((HEADS, KD, RLEN), BF),
            pltpu.VMEM((RLEN, HEADS, DC), BF),
            pltpu.VMEM((HEADS, DC, RLEN), BF),
            pltpu.VMEM((NPROMPT, SHARD, KD), BF),
            pltpu.VMEM((KEYS, KD), BF),
            pltpu.VMEM((NY - 1, SHARD, KD), BF),
            pltpu.VMEM((KEYS, COLS), F32),
            pltpu.VMEM((KEYS, COLS), F32),
            pltpu.VMEM((KEYS, COLS), F32),
            pltpu.VMEM((KEYS, COLS), F32),
            pltpu.VMEM((STEPS, KEYS, COLS), BF),
            pltpu.VMEM((STEPS, KEYS, COLS), BF),
            pltpu.VMEM((640, KEYS), F32),
            pltpu.VMEM((5, PLEN, 128), F32),
            pltpu.VMEM((NDEV * 16, 128), F32),
            pltpu.VMEM((NDEV, 16, 128), BF),
            pltpu.VMEM((NDEV, 16, 128), BF),
            pltpu.VMEM((NDEV, NDEV * 16), BF),
            pltpu.VMEM((NDEV, 128), F32),
            pltpu.SemaphoreType.DMA,
            pltpu.SemaphoreType.DMA((4,)),
            pltpu.SemaphoreType.DMA,
            pltpu.SemaphoreType.DMA((NY - 1,)),
            pltpu.SemaphoreType.DMA((NY - 1,)),
            pltpu.SemaphoreType.DMA,
            pltpu.SemaphoreType.DMA,
        ],
        compiler_params=pltpu.CompilerParams(
            collective_id=0, has_side_effects=True, vmem_limit_bytes=62 * 2 ** 20
        ),
        name="latent_grads",
    )(
        jnp.transpose(queries, (1, 2, 0)), d_output, prompt_latent, resp_latent.T,
        assignment, assignment.reshape(1, NDEV), lengths,
    )
    return jnp.transpose(dprompt, (1, 0, 2)), dresp.T


def solution(mesh):
    in_specs = (
        P(("prompt", "resp"), None, None),
        P(("prompt", "resp"), None, None),
        P(("prompt", "resp"), None),
        P(None, "prompt", None),
        P(),
        P(("prompt", "resp")),
    )
    out_specs = (P(None, ("prompt", "resp"), None), P(("prompt", "resp"), None))
    return jax.shard_map(body, mesh=mesh, in_specs=in_specs, out_specs=out_specs, check_vma=False)
```

time: 383 us -> 65.2 us (0.17)
  waiting for transfers between devices: 241 us -> 0 us
  Pallas kernels: 0 us -> 60.5 us
  matrix products: 54.2 us -> 0 us
  other arithmetic: 40.8 us -> 0 us
  local copies, waits for them, and re-layouts: 29 us -> 3.15 us
  between operations: 16.7 us -> 1.29 us
    unnamed x3 -> x0, waiting for transfers between devices: 214 us -> none
    pallas_call x0 -> x1, Pallas kernels: none -> 60.5 us  [body(): pl.pallas_call(kernel, out_shape=(jax.ShapeDtypeStruct((OWN, NPROMPT, KD)...]
    dot_general x4 -> x0, matrix products: 54.2 us -> none  [the longest x1 19.2 us: attend_grads(): jnp.einsum('ths,thk->sk', dscores, queries, preferred_element_type=jnp.fl...]
    all_gather x1 -> x0, waiting for transfers between devices: 26.6 us -> none  [body(): everything = lax.all_gather(prompt_latent, 'prompt', axis=1, tiled=True)]
    sub x2 -> x0, other arithmetic: 19.7 us -> none  [the longest x1 19.7 us: attend_grads(): expo = jnp.exp(scores - top)]
    select_n x1 -> x0, local copies, waits for them, and re-layouts: 13.2 us -> none  [attend_grads(): grads = jnp.where(live[:, None, None], d_output, jnp.zeros_like(d_output))]
    convert_element_type x1 -> x0, local copies, waits for them, and re-layouts: 12.6 us -> none  [attend_grads(): probs_b = probs.astype(jnp.bfloat16)]
    convert_element_type x2 -> x0, other arithmetic: 10.1 us -> none  [the longest x1 9.45 us: attend_grads(): probs_b = probs.astype(jnp.bfloat16)]
  transfers between devices with their start and end apart: 2 -> 0, of which waited for: 2 -> 0; matrix products, arithmetic and copies ran while one was open for 6% -> 0% of each run, Pallas kernels for 0% -> 0%
where the time goes in v1:
time: 65.2 us; the launch traced here: 65 us
  Pallas kernels  60.5 us (93%)
  local copies, waits for them, and re-layouts  3.15 us (5%)
  between operations  1.29 us (2%)
    pallas_call x1, Pallas kernels, body(): pl.pallas_call(kernel, out_shape=(jax.ShapeDtypeStruct((OWN, NPROMPT, KD)...  60.5 us
    unnamed x2, local copies, waits for them, and re-layouts  3.15 us

profile of v1, /device:TPU:1, one launch (start us, length us, event | category | flops | bytes accessed | tf_op | source)
XLA Modules:
  0.0 65.0 jit_solution(15690287673712041238)
XLA Ops:
  1.3 60.5 %latent_grads.1 = (f32[3,8,576]{2,1,0:T(8,128)}, f32[576,128]{1,0:T(8,128)}) custom-call(bf16[64,576,128]{2,1,0:T(8,128)(2,1)} %bitcast.5, bf16[128,64,512]{2,1,0:T(8,128)(2,1)} %do_hbm.1, bf16[8,96,576]{2,1,0:T(8,128)(2,1)} %prompt_hbm.1, bf16[576,128]{1,0:T(8,128)(2,1)} %bitcast.7, s32[128]{0:T(128)} %assign_ref.1, s32[1,128]{1,0:T(1,128)} %bitcast.9, ...), custom_call_target="tpu_custom_call" | custom-call | tf_op jit(solution)/shard_map/latent_grads/pallas_call | solution.py:235
  61.8 1.5 %copy.11 = f32[8,3,576]{2,0,1:T(8,128)} copy(f32[8,3,576]{2,0,1:T(8,128)} %bitcast.8) | data formatting | bytes 110592
  63.3 1.7 %copy.12 = f32[128,576]{0,1:T(8,128)} copy(f32[128,576]{0,1:T(8,128)} %bitcast.6) | data formatting | bytes 589824

commit v2 on v1

--- a/solution.py
+++ b/solution.py
@@ -29,6 +29,7 @@
 COLS = G * RLEN
 STEPS = HEADS // G
 W = 4
+UNROLL = 4
 MESH = pl.DeviceIdType.MESH
 
 
@@ -38,10 +39,6 @@
 
 NN = ((1,), (0,))
 NT = ((1,), (1,))
-
-
-def coords(device):
-    return (device // NR, lax.rem(device, NR))
 
 
 def kernel(
@@ -50,6 +47,7 @@
     q, do_v, do_t, prompt, keys, sendk, s0, s1, d0, d1, p_ref, ds_ref, acc,
     rows, msg32, msg, recv, pick, summed,
     load_sem, do_sem, prompt_sem, ksend_sem, krecv_sem, msend_sem, mrecv_sem,
+    plane_sem, cube_sem, all_sem,
 ):
     y = lax.axis_index("prompt")
     r = lax.axis_index("resp")
@@ -67,14 +65,18 @@
         do_load(g).start()
     q_load.start()
 
+    x, z, core = r // 8, lax.rem(r // 2, 4), lax.rem(r, 2)
+    y_peers = [(lax.rem(y + k, 4), r) for k in (1, 2, 3)]
+    x_peers = [(y, lax.rem(x + k, 4) * 8 + z * 2 + core) for k in (1, 2, 3)]
+    z_peers = [(y, x * 8 + lax.rem(z + k, 4) * 2 + core) for k in (1, 2, 3)]
+    core_peers = [(y, x * 8 + z * 2 + 1 - core)]
+
+    def tell(sem, peers):
+        for peer in peers:
+            pl.semaphore_signal(sem, inc=1, device_id=peer, device_id_type=MESH)
+
     barrier = pltpu.get_barrier_semaphore()
-
-    def greet(step, carry):
-        other = lax.rem(me + step, NDEV)
-        pl.semaphore_signal(barrier, inc=1, device_id=coords(other), device_id_type=MESH)
-        return carry
-
-    lax.fori_loop(1, NDEV, greet, 0)
+    tell(barrier, y_peers + x_peers + z_peers + core_peers)
 
     prompt_load.wait()
     keys[pl.ds(pl.multiple_of(y * SHARD, 16), SHARD), :] = prompt[assign_ref[me] // GROUP]
@@ -83,7 +85,7 @@
         peer = lax.rem(y + k, NY) * NR + r
         sendk[k - 1] = prompt[assign_ref[peer] // GROUP]
 
-    pl.semaphore_wait(barrier, NDEV - 1)
+    pl.semaphore_wait(barrier, 10)
 
     def key_copy(k):
         return pltpu.make_async_remote_copy(
@@ -108,6 +110,7 @@
 
     for k in (2, 1, 3):
         key_copy(k).start()
+    tell(plane_sem, x_peers)
 
     def turn(g, carry):
         do_load(g).wait()
@@ -130,6 +133,8 @@
     hit = (pid_lane == (row & 7).astype(F32)) & ((row // 8) == (lane & 15))
     pick[...] = hit.astype(BF)
 
+    pl.semaphore_wait(plane_sem, 3)
+    tell(cube_sem, z_peers)
     q_load.wait()
     for k in (1, 2, 3):
         key_arrival(k).wait_recv()
@@ -140,55 +145,75 @@
     def dcat(i):
         return jnp.concatenate([do_t[i * G + h] for h in range(G)], axis=1)
 
-    def products(i, s, d):
+    def scores(i, s):
         s[...] = dot(keys[...], qcat(i), NN)
+
+    def dprobs(i, d):
         d[...] = dot(keys[:, :DC], dcat(i), NN)
 
-    def soft(i, s_ref, d_ref):
+    def soft(i, slot, h, s_ref, d_ref):
         key_pos = lax.broadcasted_iota(jnp.int32, (RLEN, RLEN), 0)
         token = lax.broadcasted_iota(jnp.int32, (RLEN, RLEN), 1)
         allowed = key_pos <= token
         live = lax.broadcasted_iota(jnp.int32, (1, RLEN), 1) < len_ref[0]
-        for h in range(G):
-            cs = slice(h * RLEN, (h + 1) * RLEN)
-            s = s_ref[:, cs]
-            s = jnp.concatenate([s[:PLEN], jnp.where(allowed, s[PLEN:], MASKED)], axis=0)
-            top = jnp.max(s, axis=0, keepdims=True)
-            e = jnp.exp2((s - top) * EXP2_SCALE)
-            dp = d_ref[:, cs]
-            inv = 1.0 / jnp.sum(e, axis=0, keepdims=True)
-            delta = jnp.sum(e * dp, axis=0, keepdims=True) * inv
-            inv = jnp.where(live, inv, 0.0)
-            p_ref[i, :, cs] = (e * inv).astype(BF)
-            ds_ref[i, :, cs] = (e * (inv * SCALE) * (dp - delta)).astype(BF)
+        cs = slice(h * RLEN, (h + 1) * RLEN)
+        s = s_ref[:, cs]
+        s = jnp.concatenate([s[:PLEN], jnp.where(allowed, s[PLEN:], MASKED)], axis=0)
+        top = jnp.max(s, axis=0, keepdims=True)
+        e = jnp.exp2((s - top) * EXP2_SCALE)
+        dp = d_ref[:, cs]
+        inv = 1.0 / jnp.sum(e, axis=0, keepdims=True)
+        delta = jnp.sum(e * dp, axis=0, keepdims=True) * inv
+        inv = jnp.where(live, inv, 0.0)
+        p_ref[slot, :, cs] = (e * inv).astype(BF)
+        ds_ref[slot, :, cs] = (e * (inv * SCALE) * (dp - delta)).astype(BF)
 
     last = STEPS - 1
-    products(0, s0, d0)
-
-    def attend(j, carry):
-        i = 2 * j
-        products(i + 1, s1, d1)
-        soft(i, s0, d0)
-        products(jnp.minimum(i + 2, last), s0, d0)
-        soft(i + 1, s1, d1)
-        return carry
-
-    lax.fori_loop(0, STEPS // 2, attend, 0)
-
+    pl.semaphore_wait(cube_sem, 3)
+    tell(all_sem, core_peers)
     acc[...] = jnp.zeros_like(acc)
 
-    def gradients(j, carry):
-        qc = jnp.concatenate([qcat(W * j + w) for w in range(W)], axis=1)
-        dc = jnp.concatenate([dcat(W * j + w) for w in range(W)], axis=1)
-        ds = jnp.concatenate([ds_ref[W * j + w] for w in range(W)], axis=1)
-        p = jnp.concatenate([p_ref[W * j + w] for w in range(W)], axis=1)
+    def grad_k(j, n):
+        qc = jnp.concatenate([qcat(j + w) for w in range(n)], axis=1)
+        ds = jnp.concatenate([ds_ref[j + w] for w in range(n)], axis=1)
+        acc[0:KD, :] += dot(qc, ds, NT)
+
+    def grad_v(j, n):
+        dc = jnp.concatenate([dcat(j + w) for w in range(n)], axis=1)
+        p = jnp.concatenate([p_ref[j + w] for w in range(n)], axis=1)
+        acc[0:DC, :] += dot(dc, p, NT)
+
+
+    def gradients(i, n):
+        qc = jnp.concatenate([qcat(i + w) for w in range(n)], axis=1)
+        dc = jnp.concatenate([dcat(i + w) for w in range(n)], axis=1)
+        ds = jnp.concatenate([ds_ref[w] for w in range(n)], axis=1)
+        p = jnp.concatenate([p_ref[w] for w in range(n)], axis=1)
         a = dot(qc, ds, NT)
         b = dot(dc, p, NT)
         acc[0:DC, :] += a[:DC] + b
         acc[DC:KD, :] += a[DC:]
+
+    def products(i, s, d):
+        scores(i, s)
+        dprobs(i, d)
+
+    def softs(i, slot, s, d):
+        for h in range(G):
+            soft(i, slot, h, s, d)
+
+    products(0, s0, d0)
+
+    def attend(j, carry):
+        i = 2 * j
+        products(i + 1, s1, d1)
+        softs(i, 0, s0, d0)
+        products(jnp.minimum(i + 2, last), s0, d0)
+        softs(i + 1, 1, s1, d1)
+        gradients(i, 2)
         return carry
 
-    lax.fori_loop(0, STEPS // W, gradients, 0)
+    lax.fori_loop(0, STEPS // 2, attend, 0)
 
     for c in range(5):
         rows[c] = acc[c * 128:(c + 1) * 128, 0:PLEN].T
@@ -198,23 +223,33 @@
             msg32[pl.ds(i * 5 + c, NDEV, stride=16), :] = rows[c, pl.ds(i, NDEV, stride=OWN), :]
     msg[...] = msg32[...].reshape(NDEV, 16, 128).astype(BF)
 
+    pl.semaphore_wait(all_sem, 1)
+
+
+    def one(oy, other):
+        pltpu.make_async_remote_copy(
+            src_ref=msg.at[oy * NR + other], dst_ref=recv.at[me],
+            send_sem=msend_sem, recv_sem=mrecv_sem,
+            device_id=(oy, other), device_id_type=MESH,
+        ).start()
+
     def send(step, carry):
-        other = lax.rem(me + step, NDEV)
-        pltpu.make_async_remote_copy(
-            src_ref=msg.at[other], dst_ref=recv.at[me],
-            send_sem=msend_sem, recv_sem=mrecv_sem,
-            device_id=coords(other), device_id_type=MESH,
-        ).start()
+        other = lax.rem(r + step, NR)
+        for k in range(NY):
+            one(lax.rem(y + k, NY), other)
         return carry
 
-    lax.fori_loop(1, NDEV, send, 0)
+    for k in range(1, NY):
+        one(lax.rem(y + k, NY), r)
+    lax.fori_loop(1, NR, send, 0)
+
     recv[me] = msg[me]
     dresp_ref[...] = acc[0:KD, PLEN:KEYS]
 
     whole = pltpu.make_async_remote_copy(
         src_ref=msg.at[pl.ds(0, NDEV - 1)], dst_ref=recv.at[pl.ds(0, NDEV - 1)],
         send_sem=msend_sem, recv_sem=mrecv_sem,
-        device_id=coords(lax.rem(me + 1, NDEV)), device_id_type=MESH,
+        device_id=(y, lax.rem(r + 1, NR)), device_id_type=MESH,
     )
     whole.wait_recv()
     summed[...] = dot(pick[...], recv[...].reshape(NDEV * 16, 128), NN)
@@ -226,6 +261,11 @@
     whole.wait_send()
     for k in (1, 2, 3):
         key_copy(k).wait_send()
+
+
+def hand_over(dprompt_in, dresp_in, dprompt_out, dresp_out):
+    dprompt_out[...] = dprompt_in[...]
+    dresp_out[...] = dresp_in[...]
 
 
 def body(queries, d_output, resp_latent, prompt_latent, assignment, lengths):
@@ -251,8 +291,8 @@
             pltpu.VMEM((KEYS, COLS), F32),
             pltpu.VMEM((KEYS, COLS), F32),
             pltpu.VMEM((KEYS, COLS), F32),
-            pltpu.VMEM((STEPS, KEYS, COLS), BF),
-            pltpu.VMEM((STEPS, KEYS, COLS), BF),
+            pltpu.VMEM((2, KEYS, COLS), BF),
+            pltpu.VMEM((2, KEYS, COLS), BF),
             pltpu.VMEM((640, KEYS), F32),
             pltpu.VMEM((5, PLEN, 128), F32),
             pltpu.VMEM((NDEV * 16, 128), F32),
@@ -267,6 +307,9 @@
             pltpu.SemaphoreType.DMA((NY - 1,)),
             pltpu.SemaphoreType.DMA,
             pltpu.SemaphoreType.DMA,
+            pltpu.SemaphoreType.REGULAR,
+            pltpu.SemaphoreType.REGULAR,
+            pltpu.SemaphoreType.REGULAR,
         ],
         compiler_params=pltpu.CompilerParams(
             collective_id=0, has_side_effects=True, vmem_limit_bytes=62 * 2 ** 20
@@ -276,6 +319,16 @@
         jnp.transpose(queries, (1, 2, 0)), d_output, prompt_latent, resp_latent.T,
         assignment, assignment.reshape(1, NDEV), lengths,
     )
+    dprompt, dresp = pl.pallas_call(
+        hand_over,
+        out_shape=(
+            jax.ShapeDtypeStruct((OWN, NPROMPT, KD), F32),
+            jax.ShapeDtypeStruct((KD, RLEN), F32),
+        ),
+        in_specs=[vmem, vmem],
+        out_specs=(vmem, vmem),
+        name="hand_over",
+    )(dprompt, dresp)
     return jnp.transpose(dprompt, (1, 0, 2)), dresp.T
 
 

time: 65.2 us -> 57.3 us (0.88)
  Pallas kernels: 60.5 us -> 55.9 us
  local copies, waits for them, and re-layouts: 3.15 us -> 0 us
    pallas_call x1, Pallas kernels: 60.5 us -> 54.1 us  [body(): pl.pallas_call(kernel, out_shape=(jax.ShapeDtypeStruct((OWN, NPROMPT, KD)...]
    unnamed x2 -> x0, local copies, waits for them, and re-layouts: 3.15 us -> none
    pallas_call x0 -> x1, Pallas kernels: none -> 1.74 us  [body(): pl.pallas_call(hand_over, out_shape=(jax.ShapeDtypeStruct((OWN, NPROMPT,...]
where the time goes in v2:
time: 57.3 us; the launch traced here: 57.2 us
  Pallas kernels  55.9 us (98%)
  between operations  1.29 us (2%)
    pallas_call x1, Pallas kernels, body(): pl.pallas_call(kernel, out_shape=(jax.ShapeDtypeStruct((OWN, NPROMPT, KD)...  54.1 us
    pallas_call x1, Pallas kernels, body(): pl.pallas_call(hand_over, out_shape=(jax.ShapeDtypeStruct((OWN, NPROMPT,...  1.74 us

profile of v2, /device:TPU:1, one launch (start us, length us, event | category | flops | bytes accessed | tf_op | source)
XLA Modules:
  0.0 57.2 jit_solution(8072847616485765144)
XLA Ops:
  1.3 54.1 %latent_grads.1 = (f32[3,8,576]{2,1,0:T(8,128)}, f32[576,128]{1,0:T(8,128)}) custom-call(bf16[64,576,128]{2,1,0:T(8,128)(2,1)} %bitcast.5, bf16[128,64,512]{2,1,0:T(8,128)(2,1)} %do_hbm.1, bf16[8,96,576]{2,1,0:T(8,128)(2,1)} %prompt_hbm.1, bf16[576,128]{1,0:T(8,128)(2,1)} %bitcast.6, s32[128]{0:T(128)} %assign_ref.1, s32[1,128]{1,0:T(1,128)} %bitcast.7, ...), custom_call_target="tpu_custom_call" | custom-call | tf_op jit(solution)/shard_map/latent_grads/pallas_call | solution.py:275
  55.4 1.7 %hand_over.1 = (f32[3,8,576]{2,1,0:T(8,128)}, f32[576,128]{1,0:T(8,128)}) custom-call(f32[3,8,576]{2,1,0:T(8,128)} %get-tuple-element.6.dprompt_in, f32[576,128]{1,0:T(8,128)} %get-tuple-element.7.dresp_in), custom_call_target="tpu_custom_call" | custom-call | tf_op jit(solution)/shard_map/hand_over/pallas_call | solution.py:322
